TPU v7x, 32 devices: a whole 2x2x4 slice. The times are simulated.
32 devices in a mesh: seq: 8 (over z, y), chan: 4 (over x, core).
Axes of the slice: x: 2, y: 2, z: 4, core: 2. Of those that a mesh axis runs over, the one named last changes fastest.
Arguments:
- tokens: bfloat16 [2048, 4096], P('seq', 'chan'), may hold values from -6 to 6
- w_in: bfloat16 [4096, 3, 4096], P(None, None, 'chan'), may hold values from -0.09375 to 0.09375
- short_filter: float32 [3, 3, 4096], P(None, None, 'chan'), may hold values from -3 to 3
- mr_filter: bfloat16 [256, 128], P('chan'), may hold values from -0.5 to 0.5
- skip_gain: float32 [4096], P('chan'), may hold values from -4 to 4
- w_out: bfloat16 [4096, 4096], P('chan'), may hold values from -0.09375 to 0.09375
- segments: int32 [2048], replicated, may hold values from 0 to 15, never falling along the last dimension, each value on 1 to 256 neighbouring positions
Outputs:
- mixed: bfloat16 [2048, 4096], P('seq', 'chan')
Inputs may be any that keep to these rules, and one draw needn't show every extreme that they name: `segments`: document ids in contiguous sequence order never fall; each of the 16 documents holds 1 to 256 positions and one holds exactly that many.
All inputs are finite; a program needn't handle non-finite values.
Results may differ from a plain program's by a relative error of at most 0.0076.
Values may be sent and summed in bfloat16 or wider, within the bound.
A program may use at most 128 MiB of HBM per device.

v0:
```python
import functools

import jax
import jax.numpy as jnp
from jax import lax
from jax.experimental import pallas as pl
from jax.experimental.pallas import tpu as pltpu
from jax.sharding import PartitionSpec as P

LANES = 128
PACK = 16


def fold_matrix(row_count, seq_count):
    periods = row_count // (2 * seq_count)
    out_row = lax.broadcasted_iota(jnp.int32, (row_count, row_count), 0)
    in_row = lax.broadcasted_iota(jnp.int32, (row_count, row_count), 1)
    d = out_row // (2 * periods)
    a = (out_row // 2) % periods
    s = out_row % 2
    wanted = a * 2 * seq_count + jnp.where(s == 0, d, 2 * seq_count - 1 - d)
    return (wanted == in_row).astype(jnp.bfloat16)


def short_conv(x, weights, masks, start):
    rows = x.shape[0] - start
    total = weights[0:1] * x[start:]
    for j in range(1, weights.shape[0]):
        total = total + weights[j : j + 1] * x[start - j : start - j + rows] * masks[:, j : j + 1]
    return total


def mix_kernel(
    gsize, q, k, v, hq, hk, hv, short, pattern, skip, near, seg_col, seg_row, fold, out
):
    rows, lanes = q.shape
    taps = pattern.shape[1] // 2
    groups = lanes // gsize
    f32 = jnp.float32
    masks = near[...]
    qx = jnp.concatenate([hq[...].astype(f32), q[...].astype(f32)])
    kx = jnp.concatenate([hk[...].astype(f32), k[...].astype(f32)])
    vx = jnp.concatenate([hv[...].astype(f32), v[...].astype(f32)])
    sq = short_conv(qx, short[:, 0], masks[taps:], hq.shape[0])
    sk = short_conv(kx, short[:, 1], masks, hk.shape[0] - taps)
    sv = short_conv(vx, short[:, 2], masks, hk.shape[0] - taps)
    gated = (sk * sv).astype(jnp.bfloat16)
    lane_group = lax.broadcasted_iota(jnp.int32, (taps, lanes), 1) // gsize
    bands = []
    for g in range(groups):
        row = jnp.broadcast_to(pattern[g : g + 1], (taps, 2 * taps))
        bands.append(pltpu.roll(row, 0, 1, stride=1, stride_axis=0))
    parts = []
    for b in range(rows // taps):
        same = seg_col[b * taps : (b + 1) * taps] == seg_row[:, b * taps : (b + 2) * taps]
        lhs = jnp.concatenate(
            [jnp.where(same, band, 0.0).astype(jnp.bfloat16) for band in bands]
        )
        window = gated[b * taps : (b + 2) * taps]
        every = jnp.dot(lhs, window, preferred_element_type=f32)
        total = jnp.zeros((taps, lanes), f32)
        for g in range(groups):
            total = jnp.where(lane_group == g, every[g * taps : (g + 1) * taps], total)
        parts.append(total)
    long_out = jnp.concatenate(parts)
    mixed = (sq * (long_out + skip[...] * gated[taps:].astype(f32))).astype(jnp.bfloat16)
    out[...] = jnp.dot(fold[...], mixed, preferred_element_type=f32).astype(jnp.bfloat16)


def mix(qkv, halos, short_filter, mr_filter, skip_gain, segments, fold):
    rows, chans = qkv[0].shape
    groups, taps = mr_filter.shape
    short_taps = short_filter.shape[0]
    gsize = chans // groups
    per = LANES // gsize
    base = lax.axis_index("seq") * rows
    lead = halos[1].shape[0]
    padded = jnp.concatenate([jnp.full((lead,), -1, jnp.int32), segments])
    ext = lax.dynamic_slice_in_dim(padded, base, rows + lead, 0)
    window = ext[lead - taps :]
    near = jnp.stack(
        [
            (ext[lead - taps - j : rows + lead - j] == window).astype(jnp.float32)
            for j in range(short_taps)
        ],
        axis=1,
    )
    pattern = jnp.pad(mr_filter[:, ::-1].astype(jnp.float32), ((0, 0), (1, taps - 1)))
    whole = lambda shape: pl.BlockSpec(shape, lambda i: (0, 0))
    lane = lambda height: pl.BlockSpec((height, LANES), lambda i: (0, i))
    return pl.pallas_call(
        functools.partial(mix_kernel, gsize),
        grid=(chans // LANES,),
        out_shape=jax.ShapeDtypeStruct((rows, chans), jnp.bfloat16),
        in_specs=[lane(rows)] * 3
        + [lane(h.shape[0]) for h in halos]
        + [
            pl.BlockSpec((short_taps, 3, LANES), lambda i: (0, 0, i)),
            pl.BlockSpec((per, 2 * taps), lambda i: (i, 0)),
            lane(1),
            whole(near.shape),
            whole((rows, 1)),
            whole((1, rows + taps)),
            whole(fold.shape),
        ],
        out_specs=lane(rows),
        compiler_params=pltpu.CompilerParams(vmem_limit_bytes=32 * 2**20),
    )(
        *qkv,
        *halos,
        short_filter,
        pattern,
        skip_gain[None],
        near,
        ext[lead:, None],
        window[None],
        fold,
    )


def body(tokens, w_in, short_filter, mr_filter, skip_gain, w_out, segments):
    rows, width = tokens.shape
    seq_count = lax.axis_size("seq")
    taps = mr_filter.shape[1]
    fold = fold_matrix(rows, seq_count)
    pieces = tokens.reshape(seq_count, rows // seq_count, width)
    received = lax.all_to_all(pieces, "seq", split_axis=0, concat_axis=0, tiled=True)
    ordered = lax.dot_general(
        fold,
        received.reshape(rows, width),
        (((0,), (0,)), ((), ())),
        preferred_element_type=jnp.float32,
    ).astype(jnp.bfloat16)
    gathered = lax.all_gather(ordered, "chan", axis=1, tiled=True)
    q, k, v = [
        jnp.dot(gathered, w_in[:, i], preferred_element_type=jnp.float32).astype(jnp.bfloat16)
        for i in range(3)
    ]
    tails = (q[rows - PACK :], k[rows - taps - PACK :], v[rows - taps - PACK :])
    ring = [(i, i + 1) for i in range(seq_count - 1)]
    halos = lax.ppermute(tails, "seq", ring)
    folded = mix((q, k, v), halos, short_filter, mr_filter, skip_gain, segments, fold)
    outgoing = folded.reshape(seq_count, rows // seq_count, folded.shape[1])
    returned = lax.all_to_all(outgoing, "seq", split_axis=0, concat_axis=0, tiled=True)
    partial = jnp.dot(
        returned.reshape(rows, -1), w_out, preferred_element_type=jnp.float32
    ).astype(jnp.bfloat16)
    return lax.psum_scatter(partial, "chan", scatter_dimension=1, tiled=True)


def solution(mesh):
    return jax.shard_map(
        body,
        mesh=mesh,
        in_specs=(
            P("seq", "chan"),
            P(None, None, "chan"),
            P(None, None, "chan"),
            P("chan", None),
            P("chan"),
            P("chan", None),
            P(),
        ),
        out_specs=P("seq", "chan"),
        check_vma=False,
    )
```

profile of v0, /device:TPU:13, one launch (start us, length us, event | category | flops | bytes accessed | tf_op | source)
XLA Modules:
  0.0 150.7 jit_solution(15878047132142968315)
XLA Ops:
  6.5 5.7 %all-to-all-start = ((bf16[8,32,1024]{2,1,0:T(8,128)(2,1)}), bf16[8,32,1024]{2,1,0:T(8,128)(2,1)S(1)}, u32[]{:S(2)}, u32[]{:S(2)}) async-start(bf16[8,32,1024]{2,1,0:T(8,128)(2,1)} %bitcast.30), calls=%async_computation | async-start | bytes 1048576 | tf_op jit(solution)/shard_map/all_to_all | solution.py:127
  12.2 0.0 all-gather.2.cloned.1.call-start
  12.3 11.9 %all-to-all-done = bf16[8,32,1024]{2,1,0:T(8,128)(2,1)S(1)} async-done(((bf16[8,32,1024]{2,1,0:T(8,128)(2,1)}), bf16[8,32,1024]{2,1,0:T(8,128)(2,1)S(1)}, u32[]{:S(2)}, u32[]{:S(2)}) %all-to-all-start) | async-done | bytes 524320 | tf_op jit(solution)/shard_map/all_to_all | solution.py:127
  24.2 1.5 convolution_convert_fusion.1
  25.6 0.0 all-gather.2.cloned.1.call-update
  25.7 0.0 reduce-scatter.2.cloned.1.call-start
  25.7 0.8 rev.3
  26.5 0.8 pad_dynamic-slice_fusion
  27.3 0.1 fusion.22
  27.4 0.1 pad_maximum_fusion
  27.5 0.5 fusion.28.fold
  28.0 22.4 %all-gather.2.cloned.1.call-done = bf16[256,4096]{1,0:T(8,128)(2,1)} async-done(((bf16[256,1024]{1,0:T(8,128)(2,1)}), bf16[256,4096]{1,0:T(8,128)(2,1)}) %all-gather.2.cloned.1.call-update) | async-done | bytes 2097168 | tf_op jit(solution)/shard_map/all_gather | solution.py:134
  50.4 0.0 copy-start.2
  50.4 6.5 %fusion.12.k = bf16[256,1024]{1,0:T(8,128)(2,1)S(1)} fusion(bf16[256,4096]{1,0:T(8,128)(2,1)} %all-gather.2.cloned.1.call-done, bf16[4096,3,1024]{2,0,1:T(8,128)(2,1)} %param.8), kind=kOutput, calls=%fused_computation.11 | convolution fusion | flops 2147745792 | bytes 11010048 | tf_op jit(solution)/shard_map/dot_general | solution.py:136
  57.0 3.1 %collective-permute-start.1 = (bf16[144,1024]{1,0:T(8,128)(2,1)S(1)}, bf16[144,1024]{1,0:T(8,128)(2,1)S(1)}, u32[]{:S(2)}, u32[]{:S(2)}) collective-permute-start(bf16[144,1024]{1,0:T(8,128)(2,1)S(1)} %slice.42), channel_id=1, source_target_pairs={{0,4},{4,8},{8,12},{12,16},{16,20},{20,24},{24,28},{1,5},{5,9},{9,... | collective-permute-start | bytes 884744 | tf_op jit(solution)/shard_map/ppermute | solution.py:141
  60.1 0.0 copy-done.2
  60.1 5.8 %fusion.15.v = bf16[256,1024]{1,0:T(8,128)(2,1)S(1)} fusion(bf16[256,4096]{1,0:T(8,128)(2,1)S(1)} %copy-done.2, bf16[4096,3,1024]{2,0,1:T(8,128)(2,1)} %param.8), kind=kOutput, calls=%fused_computation.12 | convolution fusion | flops 2147745792 | bytes 11010048 | tf_op jit(solution)/shard_map/dot_general | solution.py:136
  65.9 0.0 copy-start
  65.9 0.0 copy-start.1
  65.9 3.2 %collective-permute-start.2 = (bf16[144,1024]{1,0:T(8,128)(2,1)S(1)}, bf16[144,1024]{1,0:T(8,128)(2,1)S(1)}, u32[]{:S(2)}, u32[]{:S(2)}) collective-permute-start(bf16[144,1024]{1,0:T(8,128)(2,1)S(1)} %slice.43), channel_id=1, source_target_pairs={{0,4},{4,8},{8,12},{12,16},{16,20},{20,24},{24,28},{1,5},{5,9},{9,... | collective-permute-start | bytes 884744 | tf_op jit(solution)/shard_map/ppermute | solution.py:141
  69.2 5.8 %fusion.9.q = bf16[256,1024]{1,0:T(8,128)(2,1)S(1)} fusion(bf16[256,4096]{1,0:T(8,128)(2,1)S(1)} %copy-done.2, bf16[4096,3,1024]{2,0,1:T(8,128)(2,1)} %param.8), kind=kOutput, calls=%fused_computation.10 | convolution fusion | flops 2147745792 | bytes 11010048 | tf_op jit(solution)/shard_map/dot_general | solution.py:136
  75.0 3.1 %collective-permute-start = (bf16[16,1024]{1,0:T(8,128)(2,1)S(1)}, bf16[16,1024]{1,0:T(8,128)(2,1)S(1)}, u32[]{:S(2)}, u32[]{:S(2)}) collective-permute-start(bf16[16,1024]{1,0:T(8,128)(2,1)S(1)} %slice.41), channel_id=1, source_target_pairs={{0,4},{4,8},{8,12},{12,16},{16,20},{20,24},{24,28},{1,5},{5,9},{9,... | collective-permute-start | bytes 98312 | tf_op jit(solution)/shard_map/ppermute | solution.py:141
  78.1 0.1 pad_convert_fusion.pattern
  78.1 0.1 slice.40
  78.2 0.1 slice.38
  78.3 0.1 copy.11.near
  78.4 0.1 copy.12.seg_col
  78.6 1.0 collective-permute-done.hq
  79.6 0.0 collective-permute-done.1.hk
  79.6 0.0 collective-permute-done.2.hv
  79.6 0.0 copy-done
  79.6 0.0 copy-done.1
  79.6 8.6 %shard_map.73 = bf16[256,1024]{1,0:T(8,128)(2,1)S(1)} custom-call(bf16[256,1024]{1,0:T(8,128)(2,1)S(1)} %fusion.9.q, bf16[256,1024]{1,0:T(8,128)(2,1)S(1)} %fusion.12.k, bf16[256,1024]{1,0:T(8,128)(2,1)S(1)} %fusion.15.v, bf16[16,1024]{1,0:T(8,128)(2,1)S(1)} %collective-permute-done.hq, bf16[144,1024]{1,0:T(8,128)(2,1)S(1)} %collective-permute-done.1.hk, ...), custom_call_target="tpu_custom_call" | custom-call | tf_op jit(solution)/shard_map/pallas_call | solution.py:91
  88.2 15.5 %all_to_all.10 = bf16[8,32,1024]{2,1,0:T(8,128)(2,1)S(1)} all-to-all(bf16[8,32,1024]{2,1,0:T(8,128)(2,1)S(1)} %bitcast.28), channel_id=1, replica_groups=mesh['seq'=8,'chan'=4] {'seq'}, dimensions={0} | all-to-all | bytes 1048576 | tf_op jit(solution)/shard_map/all_to_all | solution.py:144
  103.8 7.0 %convolution_convert_fusion = bf16[256,4096]{1,0:T(8,128)(2,1)} fusion(bf16[256,1024]{1,0:T(8,128)(2,1)S(1)} %bitcast.32, bf16[1024,4096]{1,0:T(8,128)(2,1)} %param.12), kind=kOutput, calls=%fused_computation.9 | convolution fusion | flops 2148532224 | bytes 11010048 | tf_op jit(solution)/shard_map/dot_general | solution.py:145
  110.8 0.0 reduce-scatter.2.cloned.1.call-update
  110.8 33.0 %reduce-scatter.2.cloned.1.call-done = bf16[256,1024]{1,0:T(8,128)(2,1)} async-done(((bf16[256,4096]{1,0:T(8,128)(2,1)}), bf16[256,1024]{1,0:T(8,128)(2,1)}) %reduce-scatter.2.cloned.1.call-update) | async-done | bytes 524304 | tf_op jit(solution)/shard_map/reduce_scatter | solution.py:148
  (12 shorter events, 0.1 us)
Async XLA Ops:
  6.5 17.6 %all-to-all-start = ((bf16[8,32,1024]{2,1,0:T(8,128)(2,1)}), bf16[8,32,1024]{2,1,0:T(8,128)(2,1)S(1)}, u32[]{:S(2)}, u32[]{:S(2)}) async-start(bf16[8,32,1024]{2,1,0:T(8,128)(2,1)} %bitcast.30), calls=%async_computation | async-start | bytes 1048576 | tf_op jit(solution)/shard_map/all_to_all | solution.py:127
  12.2 38.2 %all-gather.2.cloned.1.call-start = ((), (), s32[]{:S(2)}) async-start(), calls=%async_computation.3 | async-start | bytes 2621440 | tf_op jit(solution)/shard_map/all_gather | solution.py:134
  25.7 118.2 %reduce-scatter.2.cloned.1.call-start = ((), (), s32[]{:S(2)}) async-start(), calls=%async_computation.4 | async-start | bytes 2621440 | tf_op jit(solution)/shard_map/reduce_scatter | solution.py:148
  50.4 9.6 %copy-start.2 = (bf16[256,4096]{1,0:T(8,128)(2,1)S(1)}, bf16[256,4096]{1,0:T(8,128)(2,1)}, u32[]{:S(2)}) copy-start(bf16[256,4096]{1,0:T(8,128)(2,1)} %all-gather.2.cloned.1.call-done) | copy-start | bytes 6291460
  57.0 22.7 %collective-permute-start.1 = (bf16[144,1024]{1,0:T(8,128)(2,1)S(1)}, bf16[144,1024]{1,0:T(8,128)(2,1)S(1)}, u32[]{:S(2)}, u32[]{:S(2)}) collective-permute-start(bf16[144,1024]{1,0:T(8,128)(2,1)S(1)} %slice.42), channel_id=1, source_target_pairs={{0,4},{4,8},{8,12},{12,16},{16,20},{20,24},{24,28},{1,5},{5,9},{9,... | collective-permute-start | bytes 884744 | tf_op jit(solution)/shard_map/ppermute | solution.py:141
  65.9 13.7 %copy-start = (f32[3,3,1024]{2,1,0:T(4,128)S(1)}, f32[3,3,1024]{2,1,0:T(4,128)}, u32[]{:S(2)}) copy-start(f32[3,3,1024]{2,1,0:T(4,128)} %short.1) | copy-start | bytes 110596
  65.9 13.7 %copy-start.1 = (f32[1024]{0:T(1024)S(1)}, f32[1024]{0:T(1024)}, u32[]{:S(2)}) copy-start(f32[1024]{0:T(1024)} %param.11) | copy-start | bytes 12292
  65.9 13.7 %collective-permute-start.2 = (bf16[144,1024]{1,0:T(8,128)(2,1)S(1)}, bf16[144,1024]{1,0:T(8,128)(2,1)S(1)}, u32[]{:S(2)}, u32[]{:S(2)}) collective-permute-start(bf16[144,1024]{1,0:T(8,128)(2,1)S(1)} %slice.43), channel_id=1, source_target_pairs={{0,4},{4,8},{8,12},{12,16},{16,20},{20,24},{24,28},{1,5},{5,9},{9,... | collective-permute-start | bytes 884744 | tf_op jit(solution)/shard_map/ppermute | solution.py:141
  75.0 4.7 %collective-permute-start = (bf16[16,1024]{1,0:T(8,128)(2,1)S(1)}, bf16[16,1024]{1,0:T(8,128)(2,1)S(1)}, u32[]{:S(2)}, u32[]{:S(2)}) collective-permute-start(bf16[16,1024]{1,0:T(8,128)(2,1)S(1)} %slice.41), channel_id=1, source_target_pairs={{0,4},{4,8},{8,12},{12,16},{16,20},{20,24},{24,28},{1,5},{5,9},{9,... | collective-permute-start | bytes 98312 | tf_op jit(solution)/shard_map/ppermute | solution.py:141
Sparse Core Ops, SparseCore 0:
  25.8 24.5 all-gather.1
  110.9 32.8 reduce-scatter.1
where the time goes:
time: 153 us; the launch traced here: 151 us
  waiting for transfers between devices  68.4 us (45%)
  matrix products  26.6 us (17%)
  blocking collectives  15.5 us (10%)
  starting transfers between devices  15.1 us (10%)
  between operations  13.6 us (9%)
  Pallas kernels  8.57 us (6%)
  local copies, waits for them, and re-layouts  2.07 us (1%)
    reduce_scatter x1, waiting for transfers between devices, body(): return lax.psum_scatter(partial, 'chan', scatter_dimension=1, tiled=True)  33 us
    all_gather x1, waiting for transfers between devices, body(): gathered = lax.all_gather(ordered, 'chan', axis=1, tiled=True)  22.4 us
    dot_general x3, matrix products, body(): jnp.dot(gathered, w_in[:, i], preferred_element_type=jnp.float32)  18 us
    all_to_all x1, blocking collectives, body(): lax.all_to_all(outgoing, 'seq', split_axis=0, concat_axis=0, tiled=True)  15.5 us
    all_to_all x1, waiting for transfers between devices, body(): lax.all_to_all(pieces, 'seq', split_axis=0, concat_axis=0, tiled=True)  11.9 us
    ppermute x3, starting transfers between devices, body(): halos = lax.ppermute(tails, 'seq', ring)  9.44 us
    pallas_call x1, Pallas kernels, mix(): pl.pallas_call(functools.partial(mix_kernel, gsize), grid=(chans // LANES...  8.57 us
    dot_general x1, matrix products, body(): jnp.dot(returned.reshape(rows, -1), w_out, preferred_element_type=jnp.flo...  7.05 us
  transfers between devices with their start and end apart: 6, of which 4 were waited for; matrix products, arithmetic and copies ran while one was open for 10% of the time, Pallas kernels for 0%

commit v1 on v0

--- a/solution.py
+++ b/solution.py
@@ -118,11 +118,266 @@
     )
 
 
+def remote(src, dst, sems, index, device):
+    send, recv = sems
+    return pltpu.make_async_remote_copy(
+        src_ref=src,
+        dst_ref=dst,
+        send_sem=send.at[index],
+        recv_sem=recv.at[index],
+        device_id=device,
+        device_id_type=pl.DeviceIdType.MESH,
+    )
+
+
+def place(seq_count, chan_count):
+    chan = lax.axis_index("chan")
+    return lax.axis_index("seq"), chan // 2, chan % 2, chan_count // 2
+
+
+def greet(devices):
+    barrier = pltpu.get_barrier_semaphore()
+    for device in devices:
+        pl.semaphore_signal(
+            barrier, inc=1, device_id=device, device_id_type=pl.DeviceIdType.MESH
+        )
+    pl.semaphore_wait(barrier, len(devices))
+
+
+def partners(seq, chip, core, seq_count, chips):
+    rows = [{"seq": lax.rem(seq + o, seq_count)} for o in range(1, seq_count)]
+    across = [{"chan": lax.rem(chip + o, chips) * 2 + core} for o in range(1, chips)]
+    return rows, across, {"chan": chip * 2 + 1 - core}
+
+
+def exchange_rows(source, target, sems, seq, devices):
+    count = len(devices) + 1
+    piece = source.shape[0] // count
+    at = lambda ref, d: ref.at[pl.ds(pl.multiple_of(d * piece, piece), piece)]
+    copies = []
+    for o in range(1, count):
+        d = lax.rem(seq + o, count)
+        copies.append(remote(at(source, d), at(target, seq), sems, o - 1, devices[o - 1]))
+        copies[-1].start()
+    at(target, seq)[...] = at(source, seq)[...]
+    return copies
+
+
+def project_kernel(
+    seq_count, chan_count, tokens, w, order, q, k, v, hq, hk, hv,
+    landed, blocks, wbuf, total, row_send, row_recv, col_send, col_recv, halo_send, halo_recv, w_sem,
+):
+    seq, chip, core, chips = place(seq_count, chan_count)
+    rows_to, across, sibling = partners(seq, chip, core, seq_count, chips)
+    width = tokens.shape[1]
+    f32 = jnp.float32
+    tile = min(256, wbuf.shape[2])
+    tiles = wbuf.shape[2] // tile
+
+    uses = [chip * 2 + core, chip * 2 + 1 - core]
+    for o in range(1, chips):
+        origin = lax.rem(chip - o + chips, chips)
+        uses += [origin * 2 + core, origin * 2 + 1 - core]
+    part = lambda c: pl.ds(pl.multiple_of(c * width, width), width)
+    loads = []
+    for n, c in enumerate(uses):
+        loads.append(
+            pltpu.make_async_copy(w.at[:, part(c)], wbuf.at[:, part(c)], w_sem.at[n])
+        )
+        loads[-1].start()
+
+    greet(rows_to + across + [sibling])
+    copies = exchange_rows(tokens, landed, (row_send, row_recv), seq, rows_to)
+    for copy in copies:
+        copy.wait()
+    mine = uses[0]
+    blocks[mine] = jnp.dot(order[...], landed[...], preferred_element_type=f32).astype(
+        jnp.bfloat16
+    )
+    sems = (col_send, col_recv)
+    outs = [
+        remote(blocks.at[mine], blocks.at[mine], sems, o, across[o - 1])
+        for o in range(1, chips)
+    ]
+    inner = remote(blocks.at[mine], blocks.at[mine], sems, 0, sibling)
+    for copy in outs + [inner]:
+        copy.start()
+
+    def multiply(n):
+        c = uses[n]
+        loads[n].wait()
+
+        @pl.loop(0, 3 * tiles)
+        def _(t):
+            i = lax.div(t, tiles)
+            cols = pl.ds(pl.multiple_of(lax.rem(t, tiles) * tile, tile), tile)
+            term = jnp.dot(blocks[c], wbuf[i, part(c), cols], preferred_element_type=f32)
+            if n == 0:
+                total[i, :, cols] = term
+            else:
+                total[i, :, cols] += term
+
+    multiply(0)
+    inner.wait_recv()
+    multiply(1)
+    for o in range(1, chips):
+        outs[o - 1].wait_recv()
+        c = uses[2 * o]
+        forward = remote(blocks.at[c], blocks.at[c], sems, chips - 1 + o, sibling)
+        forward.start()
+        multiply(2 * o)
+        forward.wait()
+        multiply(2 * o + 1)
+    for copy in outs + [inner]:
+        copy.wait_send()
+    halos = []
+    after = rows_to[0]
+    for i, (ref, halo) in enumerate(((q, hq), (k, hk), (v, hv))):
+        ref[...] = total[i].astype(jnp.bfloat16)
+        tail = halo.shape[0]
+        src = ref.at[pl.ds(ref.shape[0] - tail, tail)]
+        halos.append(remote(src, halo, (halo_send, halo_recv), i, after))
+        halos[-1].start()
+    for copy in halos:
+        copy.wait()
+
+
+def project(tokens, w_in, order, taps, seq_count, chan_count):
+    rows, width = tokens.shape
+    chans = w_in.shape[2]
+    vmem = pl.BlockSpec(memory_space=pltpu.VMEM)
+    bf16 = jnp.bfloat16
+    dma = pltpu.SemaphoreType.DMA
+    shape = lambda height: jax.ShapeDtypeStruct((height, chans), bf16)
+    return pl.pallas_call(
+        functools.partial(project_kernel, seq_count, chan_count),
+        out_shape=[shape(rows)] * 3 + [shape(PACK)] + [shape(taps + PACK)] * 2,
+        in_specs=[vmem, pl.BlockSpec(memory_space=pl.ANY), vmem],
+        out_specs=[vmem] * 6,
+        scratch_shapes=[
+            pltpu.VMEM((rows, width), bf16),
+            pltpu.VMEM((chan_count, rows, width), bf16),
+            pltpu.VMEM((3, w_in.shape[0], chans), bf16),
+            pltpu.VMEM((3, rows, chans), jnp.float32),
+            dma((seq_count - 1,)),
+            dma((seq_count - 1,)),
+            dma((chan_count - 1,)),
+            dma((chan_count - 1,)),
+            dma((3,)),
+            dma((3,)),
+            dma((chan_count,)),
+        ],
+        compiler_params=pltpu.CompilerParams(
+            collective_id=0, has_side_effects=True, vmem_limit_bytes=48 * 2**20
+        ),
+    )(tokens, jnp.swapaxes(w_in, 0, 1), order)
+
+
+def output_kernel(
+    seq_count, chan_count, folded, w, out,
+    landed, wbuf, kept, inner_out, inner_in, across_out, across_in,
+    row_send, row_recv, inner_send, inner_recv, across_send, across_recv, w_sem,
+):
+    seq, chip, core, chips = place(seq_count, chan_count)
+    rows_to, across, sibling = partners(seq, chip, core, seq_count, chips)
+    f32 = jnp.float32
+    width = out.shape[1]
+    tile = min(256, width)
+    load = pltpu.make_async_copy(w, wbuf, w_sem)
+    load.start()
+    greet(rows_to + across + [sibling])
+    copies = exchange_rows(folded, landed, (row_send, row_recv), seq, rows_to)
+    for copy in copies:
+        copy.wait()
+    load.wait()
+
+    def multiply(c, target, slot):
+        @pl.loop(0, width // tile)
+        def _(t):
+            start = pl.multiple_of(t * tile, tile)
+            cols = pl.ds(pl.multiple_of(c * width + start, tile), tile)
+            term = jnp.dot(landed[...], wbuf[:, cols], preferred_element_type=f32)
+            target[slot, :, pl.ds(start, tile)] = term.astype(target.dtype)
+
+    inners = []
+
+    def share(c, slot):
+        multiply(c * 2 + 1 - core, inner_out, slot)
+        inners.append(
+            remote(inner_out.at[slot], inner_in.at[slot], (inner_send, inner_recv), slot, sibling)
+        )
+        inners[-1].start()
+        multiply(c * 2 + core, kept, slot)
+
+    outs = []
+    for o in range(1, chips):
+        share(lax.rem(chip + o, chips), o - 1)
+        inners[-1].wait_recv()
+        across_out[o - 1] = (kept[o - 1] + inner_in[o - 1].astype(f32)).astype(jnp.bfloat16)
+        outs.append(
+            remote(
+                across_out.at[o - 1], across_in.at[o - 1], (across_send, across_recv), o - 1,
+                across[o - 1],
+            )
+        )
+        outs[-1].start()
+    share(chip, chips - 1)
+    inners[-1].wait_recv()
+    kept[chips - 1] += inner_in[chips - 1].astype(f32)
+    result = kept[chips - 1]
+    for o in range(1, chips):
+        outs[o - 1].wait_recv()
+        result = result + across_in[o - 1].astype(f32)
+    out[...] = result.astype(out.dtype)
+    for copy in inners + outs:
+        copy.wait_send()
+
+
+def project_out(folded, w_out, seq_count, chan_count):
+    rows, chans = folded.shape
+    width = w_out.shape[1] // chan_count
+    chips = chan_count // 2
+    vmem = pl.BlockSpec(memory_space=pltpu.VMEM)
+    bf16 = jnp.bfloat16
+    dma = pltpu.SemaphoreType.DMA
+    slots = lambda count: pltpu.VMEM((count, rows, width), bf16)
+    return pl.pallas_call(
+        functools.partial(output_kernel, seq_count, chan_count),
+        out_shape=jax.ShapeDtypeStruct((rows, width), bf16),
+        in_specs=[vmem, pl.BlockSpec(memory_space=pl.ANY)],
+        out_specs=vmem,
+        scratch_shapes=[
+            pltpu.VMEM((rows, chans), bf16),
+            pltpu.VMEM(w_out.shape, bf16),
+            pltpu.VMEM((chips, rows, width), jnp.float32),
+            slots(chips),
+            slots(chips),
+            slots(chips - 1),
+            slots(chips - 1),
+            dma((seq_count - 1,)),
+            dma((seq_count - 1,)),
+            dma((chips,)),
+            dma((chips,)),
+            dma((chips - 1,)),
+            dma((chips - 1,)),
+            dma(()),
+        ],
+        compiler_params=pltpu.CompilerParams(
+            collective_id=1, has_side_effects=True, vmem_limit_bytes=32 * 2**20
+        ),
+    )(folded, w_out)
+
+
 def body(tokens, w_in, short_filter, mr_filter, skip_gain, w_out, segments):
     rows, width = tokens.shape
     seq_count = lax.axis_size("seq")
     taps = mr_filter.shape[1]
     fold = fold_matrix(rows, seq_count)
+    chan_size = lax.axis_size("chan")
+    if rows // seq_count % PACK == 0 and chan_size % 2 == 0 and chan_size > 2:
+        q, k, v, *halos = project(tokens, w_in, fold.T, taps, seq_count, chan_size)
+        folded = mix((q, k, v), halos, short_filter, mr_filter, skip_gain, segments, fold)
+        return project_out(folded, w_out, seq_count, chan_size)
     pieces = tokens.reshape(seq_count, rows // seq_count, width)
     received = lax.all_to_all(pieces, "seq", split_axis=0, concat_axis=0, tiled=True)
     ordered = lax.dot_general(

time: 153 us -> 97.3 us (0.64); the launches traced: 151 us -> 97 us
  Pallas kernels: 8.57 us -> 91.8 us
  waiting for transfers between devices: 68.4 us -> 0 us
  matrix products: 26.6 us -> 0 us
  blocking collectives: 15.5 us -> 0 us
  starting transfers between devices: 15.1 us -> 0 us
  between operations: 13.6 us -> 0.14 us
  local copies, waits for them, and re-layouts: 2.07 us -> 4.17 us
    pallas_call x0 -> x2, Pallas kernels: none -> 83.3 us  [the longest x1 49.9 us: project(): pl.pallas_call(functools.partial(project_kernel, seq_count, chan_count),...]
    reduce_scatter x1 -> x0, waiting for transfers between devices: 33 us -> none  [body(): return lax.psum_scatter(partial, 'chan', scatter_dimension=1, tiled=True)]
    dot_general x5 -> x0, matrix products: 26.6 us -> none  [the longest x3 18 us: body(): jnp.dot(gathered, w_in[:, i], preferred_element_type=jnp.float32)]
    all_gather x1 -> x0, waiting for transfers between devices: 22.4 us -> none  [body(): gathered = lax.all_gather(ordered, 'chan', axis=1, tiled=True)]
    all_to_all x1 -> x0, blocking collectives: 15.5 us -> none  [body(): lax.all_to_all(outgoing, 'seq', split_axis=0, concat_axis=0, tiled=True)]
    all_to_all x1 -> x0, waiting for transfers between devices: 11.9 us -> none  [body(): lax.all_to_all(pieces, 'seq', split_axis=0, concat_axis=0, tiled=True)]
    ppermute x3 -> x0, starting transfers between devices: 9.44 us -> none  [body(): halos = lax.ppermute(tails, 'seq', ring)]
    all_to_all x1 -> x0, starting transfers between devices: 5.66 us -> none  [body(): lax.all_to_all(pieces, 'seq', split_axis=0, concat_axis=0, tiled=True)]
  transfers between devices with their start and end apart: 6 -> 0, of which waited for: 4 -> 0; matrix products, arithmetic and copies ran while one was open for 10% -> 0% of each run, Pallas kernels for 0% -> 0%
where the time goes in v1:
time: 97.3 us; the launch traced here: 97 us
  Pallas kernels  91.8 us (94%)
  local copies, waits for them, and re-layouts  4.17 us (4%)
    pallas_call x1, Pallas kernels, project(): pl.pallas_call(functools.partial(project_kernel, seq_count, chan_count),...  49.9 us
    pallas_call x1, Pallas kernels, project_out(): pl.pallas_call(functools.partial(output_kernel, seq_count, chan_count), o...  33.4 us
    pallas_call x1, Pallas kernels, mix(): pl.pallas_call(functools.partial(mix_kernel, gsize), grid=(chans // LANES...  8.57 us
    unnamed x11, local copies, waits for them, and re-layouts  2.14 us

profile of v1, /device:TPU:13, one launch (start us, length us, event | category | flops | bytes accessed | tf_op | source)
XLA Modules:
  0.0 97.0 jit_solution(3867503385152366065)
XLA Ops:
  0.0 0.0 copy-start.2
  0.0 0.0 copy-start.1
  0.0 0.8 pad_dynamic-slice_fusion
  0.8 0.1 slice.16
  0.9 0.1 slice.14
  1.0 0.1 fusion.10
  1.1 0.1 pad_maximum_fusion
  1.2 0.8 rev.3
  2.0 0.1 pad_convert_fusion.pattern
  2.0 0.1 copy.12.seg_col
  2.2 0.1 copy.11.near
  2.3 0.0 slice-start
  2.3 0.6 fusion.8
  2.9 0.0 copy-start
  2.9 1.3 %copy-done = bf16[256,1024]{1,0:T(8,128)(2,1)S(1)} copy-done((bf16[256,1024]{1,0:T(8,128)(2,1)S(1)}, bf16[256,1024]{1,0:T(8,128)(2,1)}, u32[]{:S(2)}) %copy-start) | copy-done | bytes 524312
  4.3 0.0 slice-start.1
  4.3 49.9 %shard_map.73 = (bf16[256,1024]{1,0:T(8,128)(2,1)S(1)}, bf16[256,1024]{1,0:T(8,128)(2,1)S(1)}, bf16[256,1024]{1,0:T(8,128)(2,1)S(1)}, bf16[16,1024]{1,0:T(8,128)...) custom-call(bf16[256,1024]{1,0:T(8,128)(2,1)S(1)} %copy-done, bf16[3,4096,1024]{2,1,0:T(8,128)(2,1)} %bitcast.7, ...), custom_call_target="tpu_custom_call" | custom-call | tf_op jit(solution)/shard_map/pallas_call | solution.py:252
  54.1 0.0 copy-done.2
  54.1 0.0 copy-done.1
  54.1 8.6 %shard_map.74.folded = bf16[256,1024]{1,0:T(8,128)(2,1)S(1)} custom-call(bf16[256,1024]{1,0:T(8,128)(2,1)S(1)} %get-tuple-element.11.q, bf16[256,1024]{1,0:T(8,128)(2,1)S(1)} %get-tuple-element.12.k, bf16[256,1024]{1,0:T(8,128)(2,1)S(1)} %get-tuple-element.13.v, bf16[16,1024]{1,0:T(8,128)(2,1)S(1)} %get-tuple-element.14.hq, ...), custom_call_target="tpu_custom_call" | custom-call | tf_op jit(solution)/shard_map/pallas_call | solution.py:91
  62.7 0.0 slice-done
  62.7 0.0 slice-done.1
  62.8 33.4 %shard_map.75 = bf16[256,1024]{1,0:T(8,128)(2,1)S(1)} custom-call(bf16[256,1024]{1,0:T(8,128)(2,1)S(1)} %shard_map.74.folded, bf16[1024,4096]{1,0:T(8,128)(2,1)S(1)} %bitcast.5), custom_call_target="tpu_custom_call" | custom-call | tf_op jit(solution)/shard_map/pallas_call | solution.py:344
  96.2 0.8 copy.14
  (10 shorter events, 0.0 us)
Async XLA Ops:
  0.0 54.1 %copy-start.2 = (f32[1024]{0:T(1024)S(1)}, f32[1024]{0:T(1024)}, u32[]{:S(2)}) copy-start(f32[1024]{0:T(1024)} %param.11) | copy-start | bytes 12292
  0.0 54.1 %copy-start.1 = (f32[3,3,1024]{2,1,0:T(4,128)S(1)}, f32[3,3,1024]{2,1,0:T(4,128)}, u32[]{:S(2)}) copy-start(f32[3,3,1024]{2,1,0:T(4,128)} %short.1) | copy-start | bytes 110596
  2.3 60.4 %slice-start = ((s8[8388608]{0:T(1024)(128)(4,1)}), s8[4194304]{0:T(1024)(128)(4,1)S(1)}, s32[]{:S(2)}) async-start(s8[8388608]{0:T(1024)(128)(4,1)} %bitcast.4), calls=%async_computation | async-start | bytes 8388608
  2.9 1.3 %copy-start = (bf16[256,1024]{1,0:T(8,128)(2,1)S(1)}, bf16[256,1024]{1,0:T(8,128)(2,1)}, u32[]{:S(2)}) copy-start(bf16[256,1024]{1,0:T(8,128)(2,1)} %tokens.1) | copy-start | bytes 1572868
  4.3 58.5 %slice-start.1 = ((s8[8388608]{0:T(1024)(128)(4,1)}), s8[4194304]{0:T(1024)(128)(4,1)S(1)}, s32[]{:S(2)}) async-start(s8[8388608]{0:T(1024)(128)(4,1)} %bitcast.4), calls=%async_computation.1 | async-start | bytes 8388608

commit v2 on v1

--- a/solution.py
+++ b/solution.py
@@ -150,16 +150,21 @@
     return rows, across, {"chan": chip * 2 + 1 - core}
 
 
-def exchange_rows(source, target, sems, seq, devices):
+HALVES = (1, 0)
+
+
+def exchange_rows(source, target, sems, seq, devices, half):
     count = len(devices) + 1
     piece = source.shape[0] // count
-    at = lambda ref, d: ref.at[pl.ds(pl.multiple_of(d * piece, piece), piece)]
+    part = piece // 2
+    take = lambda d: source.at[pl.ds(pl.multiple_of(d * piece + half * part, part), part)]
+    put = target.at[half, pl.ds(pl.multiple_of(seq * part, part), part)]
     copies = []
     for o in range(1, count):
-        d = lax.rem(seq + o, count)
-        copies.append(remote(at(source, d), at(target, seq), sems, o - 1, devices[o - 1]))
+        index = half * (count - 1) + o - 1
+        copies.append(remote(take(lax.rem(seq + o, count)), put, sems, index, devices[o - 1]))
         copies[-1].start()
-    at(target, seq)[...] = at(source, seq)[...]
+    put[...] = take(seq)[...]
     return copies
 
 
@@ -169,7 +174,8 @@
 ):
     seq, chip, core, chips = place(seq_count, chan_count)
     rows_to, across, sibling = partners(seq, chip, core, seq_count, chips)
-    width = tokens.shape[1]
+    rows, width = tokens.shape
+    half_rows = rows // 2
     f32 = jnp.float32
     tile = min(256, wbuf.shape[2])
     tiles = wbuf.shape[2] // tile
@@ -187,57 +193,76 @@
         loads[-1].start()
 
     greet(rows_to + across + [sibling])
-    copies = exchange_rows(tokens, landed, (row_send, row_recv), seq, rows_to)
-    for copy in copies:
-        copy.wait()
+    row_sems = (row_send, row_recv)
+    copies = {h: exchange_rows(tokens, landed, row_sems, seq, rows_to, h) for h in HALVES}
     mine = uses[0]
-    blocks[mine] = jnp.dot(order[...], landed[...], preferred_element_type=f32).astype(
-        jnp.bfloat16
-    )
     sems = (col_send, col_recv)
-    outs = [
-        remote(blocks.at[mine], blocks.at[mine], sems, o, across[o - 1])
-        for o in range(1, chips)
-    ]
-    inner = remote(blocks.at[mine], blocks.at[mine], sems, 0, sibling)
-    for copy in outs + [inner]:
-        copy.start()
-
-    def multiply(n):
+    outs, inner = {}, {}
+
+    def spread(h):
+        for copy in copies[h]:
+            copy.wait()
+        own = blocks.at[h, mine]
+        own[...] = jnp.dot(order[...], landed[h], preferred_element_type=f32).astype(jnp.bfloat16)
+        first = h * (chan_count - 1)
+        outs[h] = [remote(own, own, sems, first + o, across[o - 1]) for o in range(1, chips)]
+        inner[h] = remote(own, own, sems, first, sibling)
+        for copy in outs[h] + [inner[h]]:
+            copy.start()
+
+    def multiply(h, n):
         c = uses[n]
-        loads[n].wait()
+        if h == HALVES[0]:
+            loads[n].wait()
 
         @pl.loop(0, 3 * tiles)
         def _(t):
             i = lax.div(t, tiles)
             cols = pl.ds(pl.multiple_of(lax.rem(t, tiles) * tile, tile), tile)
-            term = jnp.dot(blocks[c], wbuf[i, part(c), cols], preferred_element_type=f32)
+            term = jnp.dot(blocks[h, c], wbuf[i, part(c), cols], preferred_element_type=f32)
             if n == 0:
                 total[i, :, cols] = term
             else:
                 total[i, :, cols] += term
 
-    multiply(0)
-    inner.wait_recv()
-    multiply(1)
-    for o in range(1, chips):
-        outs[o - 1].wait_recv()
-        c = uses[2 * o]
-        forward = remote(blocks.at[c], blocks.at[c], sems, chips - 1 + o, sibling)
-        forward.start()
-        multiply(2 * o)
-        forward.wait()
-        multiply(2 * o + 1)
-    for copy in outs + [inner]:
-        copy.wait_send()
+    def gather(h):
+        inner[h].wait_recv()
+        multiply(h, 1)
+        for o in range(1, chips):
+            outs[h][o - 1].wait_recv()
+            own = blocks.at[h, uses[2 * o]]
+            forward = remote(own, own, sems, h * (chan_count - 1) + chips - 1 + o, sibling)
+            forward.start()
+            multiply(h, 2 * o)
+            forward.wait()
+            multiply(h, 2 * o + 1)
+        for i, ref in enumerate((q, k, v)):
+            ref[pl.ds(h * half_rows, half_rows)] = total[i].astype(jnp.bfloat16)
+
     halos = []
-    after = rows_to[0]
-    for i, (ref, halo) in enumerate(((q, hq), (k, hk), (v, hv))):
-        ref[...] = total[i].astype(jnp.bfloat16)
-        tail = halo.shape[0]
-        src = ref.at[pl.ds(ref.shape[0] - tail, tail)]
-        halos.append(remote(src, halo, (halo_send, halo_recv), i, after))
-        halos[-1].start()
+
+    def send_halo(h):
+        for i, (ref, halo) in enumerate(((q, hq), (k, hk), (v, hv))):
+            lead = rows - halo.shape[0]
+            start = max(lead, h * half_rows)
+            size = (h + 1) * half_rows - start
+            if size > 0:
+                src = ref.at[pl.ds(start, size)]
+                dst = halo.at[pl.ds(start - lead, size)]
+                halos.append(remote(src, dst, (halo_send, halo_recv), h * 3 + i, rows_to[0]))
+                halos[-1].start()
+
+    spread(1)
+    multiply(1, 0)
+    spread(0)
+    gather(1)
+    send_halo(1)
+    multiply(0, 0)
+    gather(0)
+    send_halo(0)
+    for h in HALVES:
+        for copy in outs[h] + [inner[h]]:
+            copy.wait_send()
     for copy in halos:
         copy.wait()
 
@@ -255,16 +280,16 @@
         in_specs=[vmem, pl.BlockSpec(memory_space=pl.ANY), vmem],
         out_specs=[vmem] * 6,
         scratch_shapes=[
-            pltpu.VMEM((rows, width), bf16),
-            pltpu.VMEM((chan_count, rows, width), bf16),
+            pltpu.VMEM((2, rows // 2, width), bf16),
+            pltpu.VMEM((2, chan_count, rows // 2, width), bf16),
             pltpu.VMEM((3, w_in.shape[0], chans), bf16),
-            pltpu.VMEM((3, rows, chans), jnp.float32),
-            dma((seq_count - 1,)),
-            dma((seq_count - 1,)),
-            dma((chan_count - 1,)),
-            dma((chan_count - 1,)),
-            dma((3,)),
-            dma((3,)),
+            pltpu.VMEM((3, rows // 2, chans), jnp.float32),
+            dma((2 * (seq_count - 1),)),
+            dma((2 * (seq_count - 1),)),
+            dma((2 * (chan_count - 1),)),
+            dma((2 * (chan_count - 1),)),
+            dma((6,)),
+            dma((6,)),
             dma((chan_count,)),
         ],
         compiler_params=pltpu.CompilerParams(
@@ -286,51 +311,56 @@
     load = pltpu.make_async_copy(w, wbuf, w_sem)
     load.start()
     greet(rows_to + across + [sibling])
-    copies = exchange_rows(folded, landed, (row_send, row_recv), seq, rows_to)
-    for copy in copies:
-        copy.wait()
-    load.wait()
-
-    def multiply(c, target, slot):
+    row_sems = (row_send, row_recv)
+    copies = {h: exchange_rows(folded, landed, row_sems, seq, rows_to, h) for h in HALVES}
+
+    def multiply(h, c, target, slot):
         @pl.loop(0, width // tile)
         def _(t):
             start = pl.multiple_of(t * tile, tile)
             cols = pl.ds(pl.multiple_of(c * width + start, tile), tile)
-            term = jnp.dot(landed[...], wbuf[:, cols], preferred_element_type=f32)
-            target[slot, :, pl.ds(start, tile)] = term.astype(target.dtype)
-
-    inners = []
-
-    def share(c, slot):
-        multiply(c * 2 + 1 - core, inner_out, slot)
-        inners.append(
-            remote(inner_out.at[slot], inner_in.at[slot], (inner_send, inner_recv), slot, sibling)
-        )
-        inners[-1].start()
-        multiply(c * 2 + core, kept, slot)
-
-    outs = []
-    for o in range(1, chips):
-        share(lax.rem(chip + o, chips), o - 1)
-        inners[-1].wait_recv()
-        across_out[o - 1] = (kept[o - 1] + inner_in[o - 1].astype(f32)).astype(jnp.bfloat16)
-        outs.append(
-            remote(
-                across_out.at[o - 1], across_in.at[o - 1], (across_send, across_recv), o - 1,
-                across[o - 1],
-            )
-        )
-        outs[-1].start()
-    share(chip, chips - 1)
-    inners[-1].wait_recv()
-    kept[chips - 1] += inner_in[chips - 1].astype(f32)
-    result = kept[chips - 1]
-    for o in range(1, chips):
-        outs[o - 1].wait_recv()
-        result = result + across_in[o - 1].astype(f32)
-    out[...] = result.astype(out.dtype)
-    for copy in inners + outs:
-        copy.wait_send()
+            term = jnp.dot(landed[h], wbuf[:, cols], preferred_element_type=f32)
+            target[h, slot, :, pl.ds(start, tile)] = term.astype(target.dtype)
+
+    inners, outs = {0: [], 1: []}, {0: [], 1: []}
+
+    def share(h, c, slot):
+        multiply(h, c * 2 + 1 - core, inner_out, slot)
+        src, dst = inner_out.at[h, slot], inner_in.at[h, slot]
+        index = h * chips + slot
+        inners[h].append(remote(src, dst, (inner_send, inner_recv), index, sibling))
+        inners[h][-1].start()
+        multiply(h, c * 2 + core, kept, slot)
+
+    for h in HALVES:
+        for copy in copies[h]:
+            copy.wait()
+        if h == HALVES[0]:
+            load.wait()
+        for o in range(1, chips):
+            n = o - 1
+            share(h, lax.rem(chip + o, chips), n)
+            inners[h][-1].wait_recv()
+            across_out[h, n] = (kept[h, n] + inner_in[h, n].astype(f32)).astype(jnp.bfloat16)
+            src, dst = across_out.at[h, n], across_in.at[h, n]
+            index = h * (chips - 1) + n
+            outs[h].append(remote(src, dst, (across_send, across_recv), index, across[n]))
+            outs[h][-1].start()
+        share(h, chip, chips - 1)
+
+    part = landed.shape[1] // seq_count
+    for h in HALVES:
+        inners[h][-1].wait_recv()
+        result = kept[h, chips - 1] + inner_in[h, chips - 1].astype(f32)
+        for o in range(1, chips):
+            outs[h][o - 1].wait_recv()
+            result = result + across_in[h, o - 1].astype(f32)
+        result = result.astype(out.dtype)
+        for d in range(seq_count):
+            out[pl.ds((2 * d + h) * part, part)] = result[d * part : (d + 1) * part]
+    for h in HALVES:
+        for copy in inners[h] + outs[h]:
+            copy.wait_send()
 
 
 def project_out(folded, w_out, seq_count, chan_count):
@@ -340,26 +370,26 @@
     vmem = pl.BlockSpec(memory_space=pltpu.VMEM)
     bf16 = jnp.bfloat16
     dma = pltpu.SemaphoreType.DMA
-    slots = lambda count: pltpu.VMEM((count, rows, width), bf16)
+    slots = lambda count: pltpu.VMEM((2, count, rows // 2, width), bf16)
     return pl.pallas_call(
         functools.partial(output_kernel, seq_count, chan_count),
         out_shape=jax.ShapeDtypeStruct((rows, width), bf16),
         in_specs=[vmem, pl.BlockSpec(memory_space=pl.ANY)],
         out_specs=vmem,
         scratch_shapes=[
-            pltpu.VMEM((rows, chans), bf16),
+            pltpu.VMEM((2, rows // 2, chans), bf16),
             pltpu.VMEM(w_out.shape, bf16),
-            pltpu.VMEM((chips, rows, width), jnp.float32),
+            pltpu.VMEM((2, chips, rows // 2, width), jnp.float32),
             slots(chips),
             slots(chips),
             slots(chips - 1),
             slots(chips - 1),
-            dma((seq_count - 1,)),
-            dma((seq_count - 1,)),
-            dma((chips,)),
-            dma((chips,)),
-            dma((chips - 1,)),
-            dma((chips - 1,)),
+            dma((2 * (seq_count - 1),)),
+            dma((2 * (seq_count - 1),)),
+            dma((2 * chips,)),
+            dma((2 * chips,)),
+            dma((2 * (chips - 1),)),
+            dma((2 * (chips - 1),)),
             dma(()),
         ],
         compiler_params=pltpu.CompilerParams(
@@ -374,8 +404,8 @@
     taps = mr_filter.shape[1]
     fold = fold_matrix(rows, seq_count)
     chan_size = lax.axis_size("chan")
-    if rows // seq_count % PACK == 0 and chan_size % 2 == 0 and chan_size > 2:
-        q, k, v, *halos = project(tokens, w_in, fold.T, taps, seq_count, chan_size)
+    if rows // seq_count % (2 * PACK) == 0 and chan_size % 2 == 0 and chan_size > 2:
+        q, k, v, *halos = project(tokens, w_in, fold_matrix(rows // 2, seq_count).T, taps, seq_count, chan_size)
         folded = mix((q, k, v), halos, short_filter, mr_filter, skip_gain, segments, fold)
         return project_out(folded, w_out, seq_count, chan_size)
     pieces = tokens.reshape(seq_count, rows // seq_count, width)

time: 97.3 us -> 88.7 us (0.912)
  Pallas kernels: 91.8 us -> 83 us
    pallas_call x1, Pallas kernels: 49.9 us -> 41.2 us  [project(): pl.pallas_call(functools.partial(project_kernel, seq_count, chan_count),...]
    unnamed x11 -> x9, local copies, waits for them, and re-layouts: 2.14 us -> 1.85 us
where the time goes in v2:
time: 88.7 us; the launch traced here: 87.8 us
  Pallas kernels  83 us (94%)
  local copies, waits for them, and re-layouts  3.87 us (4%)
    pallas_call x1, Pallas kernels, project(): pl.pallas_call(functools.partial(project_kernel, seq_count, chan_count),...  41.2 us
    pallas_call x1, Pallas kernels, project_out(): pl.pallas_call(functools.partial(output_kernel, seq_count, chan_count), o...  33.2 us
    pallas_call x1, Pallas kernels, mix(): pl.pallas_call(functools.partial(mix_kernel, gsize), grid=(chans // LANES...  8.57 us
    unnamed x9, local copies, waits for them, and re-layouts  1.85 us

profile of v2, /device:TPU:13, one launch (start us, length us, event | category | flops | bytes accessed | tf_op | source)
XLA Modules:
  0.0 87.8 jit_solution(12902880191917796130)
XLA Ops:
  0.0 0.0 copy-start.3
  0.0 0.0 copy-start.2
  0.1 0.8 pad_dynamic-slice_fusion
  0.9 0.1 slice.16
  1.0 0.1 slice.14
  1.0 0.1 fusion.10
  1.1 0.1 pad_maximum_fusion
  1.2 0.8 rev.3
  2.0 0.1 pad_convert_fusion.pattern
  2.1 0.5 fusion.4.fold
  2.7 0.1 copy.12.seg_col
  2.8 0.1 copy.11.near
  3.0 0.0 copy-start.1
  3.0 1.0 %copy-done.1 = bf16[256,1024]{1,0:T(8,128)(2,1)S(1)} copy-done((bf16[256,1024]{1,0:T(8,128)(2,1)S(1)}, bf16[256,1024]{1,0:T(8,128)(2,1)}, u32[]{:S(2)}) %copy-start.1) | copy-done | bytes 524312
  4.0 0.0 copy-start
  4.0 41.2 %shard_map.73 = (bf16[256,1024]{1,0:T(8,128)(2,1)S(1)}, bf16[256,1024]{1,0:T(8,128)(2,1)S(1)}, bf16[256,1024]{1,0:T(8,128)(2,1)S(1)}, bf16[16,1024]{1,0:T(8,128)...) custom-call(bf16[256,1024]{1,0:T(8,128)(2,1)S(1)} %copy-done.1, bf16[3,4096,1024]{2,1,0:T(8,128)(2,1)} %bitcast.5, ...), custom_call_target="tpu_custom_call" | custom-call | tf_op jit(solution)/shard_map/pallas_call | solution.py:277
  45.2 0.0 copy-done.3
  45.2 0.0 copy-done.2
  45.2 8.6 %shard_map.74.folded = bf16[256,1024]{1,0:T(8,128)(2,1)S(1)} custom-call(bf16[256,1024]{1,0:T(8,128)(2,1)S(1)} %get-tuple-element.11.q, bf16[256,1024]{1,0:T(8,128)(2,1)S(1)} %get-tuple-element.12.k, bf16[256,1024]{1,0:T(8,128)(2,1)S(1)} %get-tuple-element.13.v, bf16[16,1024]{1,0:T(8,128)(2,1)S(1)} %get-tuple-element.14.hq, ...), custom_call_target="tpu_custom_call" | custom-call | tf_op jit(solution)/shard_map/pallas_call | solution.py:91
  53.8 0.0 copy-done
  53.8 33.2 %shard_map.75 = bf16[256,1024]{1,0:T(8,128)(2,1)S(1)} custom-call(bf16[256,1024]{1,0:T(8,128)(2,1)S(1)} %shard_map.74.folded, bf16[1024,4096]{1,0:T(8,128)(2,1)S(1)} %copy-done), custom_call_target="tpu_custom_call" | custom-call | tf_op jit(solution)/shard_map/pallas_call | solution.py:374
  87.0 0.8 copy.14
  (15 shorter events, 0.1 us)
Async XLA Ops:
  0.0 45.2 %copy-start.3 = (f32[1024]{0:T(1024)S(1)}, f32[1024]{0:T(1024)}, u32[]{:S(2)}) copy-start(f32[1024]{0:T(1024)} %param.11) | copy-start | bytes 12292
  0.0 45.2 %copy-start.2 = (f32[3,3,1024]{2,1,0:T(4,128)S(1)}, f32[3,3,1024]{2,1,0:T(4,128)}, u32[]{:S(2)}) copy-start(f32[3,3,1024]{2,1,0:T(4,128)} %short.1) | copy-start | bytes 110596
  3.0 1.0 %copy-start.1 = (bf16[256,1024]{1,0:T(8,128)(2,1)S(1)}, bf16[256,1024]{1,0:T(8,128)(2,1)}, u32[]{:S(2)}) copy-start(bf16[256,1024]{1,0:T(8,128)(2,1)} %tokens.1) | copy-start | bytes 1572868
  4.0 49.8 %copy-start = (bf16[1024,4096]{1,0:T(8,128)(2,1)S(1)}, bf16[1024,4096]{1,0:T(8,128)(2,1)}, u32[]{:S(2)}) copy-start(bf16[1024,4096]{1,0:T(8,128)(2,1)} %w.1) | copy-start | bytes 25165828

commit v3 on v2

--- a/solution.py
+++ b/solution.py
@@ -199,10 +199,12 @@
     sems = (col_send, col_recv)
     outs, inner = {}, {}
 
+    block = lambda c, h: blocks.at[c, pl.ds(h * half_rows, half_rows)]
+
     def spread(h):
         for copy in copies[h]:
             copy.wait()
-        own = blocks.at[h, mine]
+        own = block(mine, h)
         own[...] = jnp.dot(order[...], landed[h], preferred_element_type=f32).astype(jnp.bfloat16)
         first = h * (chan_count - 1)
         outs[h] = [remote(own, own, sems, first + o, across[o - 1]) for o in range(1, chips)]
@@ -210,56 +212,54 @@
         for copy in outs[h] + [inner[h]]:
             copy.start()
 
-    def multiply(h, n):
+    def multiply(n, i, target=None):
         c = uses[n]
-        if h == HALVES[0]:
-            loads[n].wait()
-
-        @pl.loop(0, 3 * tiles)
+
+        @pl.loop(0, tiles)
         def _(t):
-            i = lax.div(t, tiles)
-            cols = pl.ds(pl.multiple_of(lax.rem(t, tiles) * tile, tile), tile)
-            term = jnp.dot(blocks[h, c], wbuf[i, part(c), cols], preferred_element_type=f32)
-            if n == 0:
+            cols = pl.ds(pl.multiple_of(t * tile, tile), tile)
+            term = jnp.dot(blocks[c], wbuf[i, part(c), cols], preferred_element_type=f32)
+            if n > 0:
+                term += total[i, :, cols]
+            if target is None:
                 total[i, :, cols] = term
             else:
-                total[i, :, cols] += term
-
-    def gather(h):
-        inner[h].wait_recv()
-        multiply(h, 1)
-        for o in range(1, chips):
+                target[:, cols] = term.astype(jnp.bfloat16)
+
+    def forward(o):
+        copies = []
+        for h in HALVES:
             outs[h][o - 1].wait_recv()
-            own = blocks.at[h, uses[2 * o]]
-            forward = remote(own, own, sems, h * (chan_count - 1) + chips - 1 + o, sibling)
-            forward.start()
-            multiply(h, 2 * o)
-            forward.wait()
-            multiply(h, 2 * o + 1)
-        for i, ref in enumerate((q, k, v)):
-            ref[pl.ds(h * half_rows, half_rows)] = total[i].astype(jnp.bfloat16)
-
+            ref = block(uses[2 * o], h)
+            index = h * (chan_count - 1) + chips - 1 + o
+            copies.append(remote(ref, ref, sems, index, sibling))
+            copies[-1].start()
+        return copies
+
+    for h in HALVES:
+        spread(h)
+    last = chan_count - 1
+    forwards = []
     halos = []
-
-    def send_halo(h):
-        for i, (ref, halo) in enumerate(((q, hq), (k, hk), (v, hv))):
-            lead = rows - halo.shape[0]
-            start = max(lead, h * half_rows)
-            size = (h + 1) * half_rows - start
-            if size > 0:
-                src = ref.at[pl.ds(start, size)]
-                dst = halo.at[pl.ds(start - lead, size)]
-                halos.append(remote(src, dst, (halo_send, halo_recv), h * 3 + i, rows_to[0]))
-                halos[-1].start()
-
-    spread(1)
-    multiply(1, 0)
-    spread(0)
-    gather(1)
-    send_halo(1)
-    multiply(0, 0)
-    gather(0)
-    send_halo(0)
+    for n in range(chan_count):
+        loads[n].wait()
+        if n == 1:
+            for h in HALVES:
+                inner[h].wait_recv()
+        elif n > 1 and n % 2 == 0:
+            forwards = forward(n // 2)
+        elif n > 1:
+            for copy in forwards:
+                copy.wait()
+        if n < last:
+            for i in range(3):
+                multiply(n, i)
+    for i, ref, halo in ((1, k, hk), (2, v, hv), (0, q, hq)):
+        multiply(last, i, ref)
+        tail = halo.shape[0]
+        src = ref.at[pl.ds(rows - tail, tail)]
+        halos.append(remote(src, halo, (halo_send, halo_recv), i, rows_to[0]))
+        halos[-1].start()
     for h in HALVES:
         for copy in outs[h] + [inner[h]]:
             copy.wait_send()
@@ -281,15 +281,15 @@
         out_specs=[vmem] * 6,
         scratch_shapes=[
             pltpu.VMEM((2, rows // 2, width), bf16),
-            pltpu.VMEM((2, chan_count, rows // 2, width), bf16),
+            pltpu.VMEM((chan_count, rows, width), bf16),
             pltpu.VMEM((3, w_in.shape[0], chans), bf16),
-            pltpu.VMEM((3, rows // 2, chans), jnp.float32),
+            pltpu.VMEM((3, rows, chans), jnp.float32),
             dma((2 * (seq_count - 1),)),
             dma((2 * (seq_count - 1),)),
             dma((2 * (chan_count - 1),)),
             dma((2 * (chan_count - 1),)),
-            dma((6,)),
-            dma((6,)),
+            dma((3,)),
+            dma((3,)),
             dma((chan_count,)),
         ],
         compiler_params=pltpu.CompilerParams(
@@ -314,23 +314,29 @@
     row_sems = (row_send, row_recv)
     copies = {h: exchange_rows(folded, landed, row_sems, seq, rows_to, h) for h in HALVES}
 
-    def multiply(h, c, target, slot):
+    half_rows = landed.shape[1]
+
+    def multiply(halves, c, target, slot):
         @pl.loop(0, width // tile)
         def _(t):
             start = pl.multiple_of(t * tile, tile)
             cols = pl.ds(pl.multiple_of(c * width + start, tile), tile)
-            term = jnp.dot(landed[h], wbuf[:, cols], preferred_element_type=f32)
-            target[h, slot, :, pl.ds(start, tile)] = term.astype(target.dtype)
+            lhs = jnp.concatenate([landed[h] for h in halves])
+            term = jnp.dot(lhs, wbuf[:, cols], preferred_element_type=f32).astype(target.dtype)
+            for n, h in enumerate(halves):
+                rows = term[n * half_rows : (n + 1) * half_rows]
+                target[h, slot, :, pl.ds(start, tile)] = rows
 
     inners, outs = {0: [], 1: []}, {0: [], 1: []}
 
-    def share(h, c, slot):
-        multiply(h, c * 2 + 1 - core, inner_out, slot)
-        src, dst = inner_out.at[h, slot], inner_in.at[h, slot]
-        index = h * chips + slot
-        inners[h].append(remote(src, dst, (inner_send, inner_recv), index, sibling))
-        inners[h][-1].start()
-        multiply(h, c * 2 + core, kept, slot)
+    def share(halves, c, slot):
+        multiply(halves, c * 2 + 1 - core, inner_out, slot)
+        for h in halves:
+            src, dst = inner_out.at[h, slot], inner_in.at[h, slot]
+            index = h * chips + slot
+            inners[h].append(remote(src, dst, (inner_send, inner_recv), index, sibling))
+            inners[h][-1].start()
+        multiply(halves, c * 2 + core, kept, slot)
 
     for h in HALVES:
         for copy in copies[h]:
@@ -339,14 +345,14 @@
             load.wait()
         for o in range(1, chips):
             n = o - 1
-            share(h, lax.rem(chip + o, chips), n)
+            share((h,), lax.rem(chip + o, chips), n)
             inners[h][-1].wait_recv()
             across_out[h, n] = (kept[h, n] + inner_in[h, n].astype(f32)).astype(jnp.bfloat16)
             src, dst = across_out.at[h, n], across_in.at[h, n]
             index = h * (chips - 1) + n
             outs[h].append(remote(src, dst, (across_send, across_recv), index, across[n]))
             outs[h][-1].start()
-        share(h, chip, chips - 1)
+    share(HALVES, chip, chips - 1)
 
     part = landed.shape[1] // seq_count
     for h in HALVES:

time: 88.7 us -> 88.7 us (level)
    pallas_call x1, Pallas kernels: 41.2 us -> 44.3 us  [project(): pl.pallas_call(functools.partial(project_kernel, seq_count, chan_count),...]
    pallas_call x1, Pallas kernels: 33.2 us -> 30.8 us  [project_out(): pl.pallas_call(functools.partial(output_kernel, seq_count, chan_count), o...]
where the time goes in v3:
time: 88.7 us; the launch traced here: 88.5 us
  Pallas kernels  83.6 us (94%)
  local copies, waits for them, and re-layouts  3.87 us (4%)
    pallas_call x1, Pallas kernels, project(): pl.pallas_call(functools.partial(project_kernel, seq_count, chan_count),...  44.3 us
    pallas_call x1, Pallas kernels, project_out(): pl.pallas_call(functools.partial(output_kernel, seq_count, chan_count), o...  30.8 us
    pallas_call x1, Pallas kernels, mix(): pl.pallas_call(functools.partial(mix_kernel, gsize), grid=(chans // LANES...  8.56 us
    unnamed x9, local copies, waits for them, and re-layouts  1.85 us

profile of v3, /device:TPU:13, one launch (start us, length us, event | category | flops | bytes accessed | tf_op | source)
XLA Modules:
  0.0 88.5 jit_solution(2473739736169302038)
XLA Ops:
  0.0 0.0 copy-start.3
  0.0 0.0 copy-start.2
  0.1 0.8 pad_dynamic-slice_fusion
  0.9 0.1 slice.16
  1.0 0.1 slice.14
  1.0 0.1 fusion.10
  1.1 0.1 pad_maximum_fusion
  1.2 0.8 rev.3
  2.0 0.1 pad_convert_fusion.pattern
  2.1 0.5 fusion.4.fold
  2.7 0.1 copy.12.seg_col
  2.8 0.1 copy.11.near
  3.0 0.0 copy-start.1
  3.0 1.0 %copy-done.1 = bf16[256,1024]{1,0:T(8,128)(2,1)S(1)} copy-done((bf16[256,1024]{1,0:T(8,128)(2,1)S(1)}, bf16[256,1024]{1,0:T(8,128)(2,1)}, u32[]{:S(2)}) %copy-start.1) | copy-done | bytes 524312
  4.0 0.0 copy-start
  4.0 44.3 %shard_map.73 = (bf16[256,1024]{1,0:T(8,128)(2,1)S(1)}, bf16[256,1024]{1,0:T(8,128)(2,1)S(1)}, bf16[256,1024]{1,0:T(8,128)(2,1)S(1)}, bf16[16,1024]{1,0:T(8,128)...) custom-call(bf16[256,1024]{1,0:T(8,128)(2,1)S(1)} %copy-done.1, bf16[3,4096,1024]{2,1,0:T(8,128)(2,1)} %bitcast.5, ...), custom_call_target="tpu_custom_call" | custom-call | tf_op jit(solution)/shard_map/pallas_call | solution.py:277
  48.3 0.0 copy-done.3
  48.3 0.0 copy-done.2
  48.3 8.6 %shard_map.74.folded = bf16[256,1024]{1,0:T(8,128)(2,1)S(1)} custom-call(bf16[256,1024]{1,0:T(8,128)(2,1)S(1)} %get-tuple-element.11.q, bf16[256,1024]{1,0:T(8,128)(2,1)S(1)} %get-tuple-element.12.k, bf16[256,1024]{1,0:T(8,128)(2,1)S(1)} %get-tuple-element.13.v, bf16[16,1024]{1,0:T(8,128)(2,1)S(1)} %get-tuple-element.14.hq, ...), custom_call_target="tpu_custom_call" | custom-call | tf_op jit(solution)/shard_map/pallas_call | solution.py:91
  56.9 0.0 copy-done
  56.9 30.8 %shard_map.75 = bf16[256,1024]{1,0:T(8,128)(2,1)S(1)} custom-call(bf16[256,1024]{1,0:T(8,128)(2,1)S(1)} %shard_map.74.folded, bf16[1024,4096]{1,0:T(8,128)(2,1)S(1)} %copy-done), custom_call_target="tpu_custom_call" | custom-call | tf_op jit(solution)/shard_map/pallas_call | solution.py:380
  87.7 0.8 copy.14
  (15 shorter events, 0.1 us)
Async XLA Ops:
  0.0 48.3 %copy-start.3 = (f32[1024]{0:T(1024)S(1)}, f32[1024]{0:T(1024)}, u32[]{:S(2)}) copy-start(f32[1024]{0:T(1024)} %param.11) | copy-start | bytes 12292
  0.0 48.3 %copy-start.2 = (f32[3,3,1024]{2,1,0:T(4,128)S(1)}, f32[3,3,1024]{2,1,0:T(4,128)}, u32[]{:S(2)}) copy-start(f32[3,3,1024]{2,1,0:T(4,128)} %short.1) | copy-start | bytes 110596
  3.0 1.0 %copy-start.1 = (bf16[256,1024]{1,0:T(8,128)(2,1)S(1)}, bf16[256,1024]{1,0:T(8,128)(2,1)}, u32[]{:S(2)}) copy-start(bf16[256,1024]{1,0:T(8,128)(2,1)} %tokens.1) | copy-start | bytes 1572868
  4.0 52.9 %copy-start = (bf16[1024,4096]{1,0:T(8,128)(2,1)S(1)}, bf16[1024,4096]{1,0:T(8,128)(2,1)}, u32[]{:S(2)}) copy-start(bf16[1024,4096]{1,0:T(8,128)(2,1)} %w.1) | copy-start | bytes 25165828

commit v4 on v3

--- a/solution.py
+++ b/solution.py
@@ -212,54 +212,67 @@
         for copy in outs[h] + [inner[h]]:
             copy.start()
 
-    def multiply(n, i, target=None):
+    last = chan_count - 1
+
+    def multiply(n, i, span, target):
         c = uses[n]
 
         @pl.loop(0, tiles)
         def _(t):
             cols = pl.ds(pl.multiple_of(t * tile, tile), tile)
-            term = jnp.dot(blocks[c], wbuf[i, part(c), cols], preferred_element_type=f32)
+            term = jnp.dot(blocks[c, span], wbuf[i, part(c), cols], preferred_element_type=f32)
             if n > 0:
-                term += total[i, :, cols]
-            if target is None:
-                total[i, :, cols] = term
+                term += total[i, span, cols]
+            if n < last:
+                total[i, span, cols] = term
             else:
-                target[:, cols] = term.astype(jnp.bfloat16)
-
-    def forward(o):
-        copies = []
-        for h in HALVES:
-            outs[h][o - 1].wait_recv()
-            ref = block(uses[2 * o], h)
-            index = h * (chan_count - 1) + chips - 1 + o
-            copies.append(remote(ref, ref, sems, index, sibling))
-            copies[-1].start()
-        return copies
-
-    for h in HALVES:
-        spread(h)
-    last = chan_count - 1
-    forwards = []
+                target[span, cols] = term.astype(jnp.bfloat16)
+
+    forwards = {}
+
+    def arrive(h, n):
+        if n == 1:
+            inner[h].wait_recv()
+        elif n > 1 and n % 2 == 0:
+            outs[h][n // 2 - 1].wait_recv()
+            ref = block(uses[n], h)
+            index = h * (chan_count - 1) + chips - 1 + n // 2
+            forwards[h, n] = remote(ref, ref, sems, index, sibling)
+            forwards[h, n].start()
+        elif n > 1:
+            forwards[h, n - 1].wait()
+
     halos = []
+
+    def send_halo(i, ref, halo, h):
+        lead = rows - halo.shape[0]
+        start = max(lead, h * half_rows)
+        size = (h + 1) * half_rows - start
+        if size > 0:
+            src = ref.at[pl.ds(start, size)]
+            dst = halo.at[pl.ds(start - lead, size)]
+            halos.append(remote(src, dst, (halo_send, halo_recv), h * 3 + i, rows_to[0]))
+            halos[-1].start()
+
+    pair = ((1, k, hk), (2, v, hv))
+    spread(1)
     for n in range(chan_count):
         loads[n].wait()
-        if n == 1:
-            for h in HALVES:
-                inner[h].wait_recv()
-        elif n > 1 and n % 2 == 0:
-            forwards = forward(n // 2)
-        elif n > 1:
-            for copy in forwards:
-                copy.wait()
-        if n < last:
-            for i in range(3):
-                multiply(n, i)
-    for i, ref, halo in ((1, k, hk), (2, v, hv), (0, q, hq)):
-        multiply(last, i, ref)
-        tail = halo.shape[0]
-        src = ref.at[pl.ds(rows - tail, tail)]
-        halos.append(remote(src, halo, (halo_send, halo_recv), i, rows_to[0]))
-        halos[-1].start()
+        arrive(1, n)
+        for i, ref, halo in pair:
+            multiply(n, i, pl.ds(half_rows, half_rows), ref)
+            if n == last:
+                send_halo(i, ref, halo, 1)
+        if n == 0:
+            spread(0)
+    for n in range(chan_count):
+        arrive(0, n)
+        multiply(n, 0, pl.ds(0, rows), q)
+    send_halo(0, q, hq, 1)
+    for i, ref, halo in pair:
+        for n in range(chan_count):
+            multiply(n, i, pl.ds(0, half_rows), ref)
+        send_halo(i, ref, halo, 0)
     for h in HALVES:
         for copy in outs[h] + [inner[h]]:
             copy.wait_send()
@@ -288,8 +301,8 @@
             dma((2 * (seq_count - 1),)),
             dma((2 * (chan_count - 1),)),
             dma((2 * (chan_count - 1),)),
-            dma((3,)),
-            dma((3,)),
+            dma((6,)),
+            dma((6,)),
             dma((chan_count,)),
         ],
         compiler_params=pltpu.CompilerParams(

time: 88.7 us -> 88.2 us (level)
    pallas_call x1, Pallas kernels: 44.3 us -> 41.4 us  [project(): pl.pallas_call(functools.partial(project_kernel, seq_count, chan_count),...]
    pallas_call x1, Pallas kernels: 30.8 us -> 32.8 us  [project_out(): pl.pallas_call(functools.partial(output_kernel, seq_count, chan_count), o...]
where the time goes in v4:
time: 88.2 us; the launch traced here: 87.7 us
  Pallas kernels  82.8 us (94%)
  local copies, waits for them, and re-layouts  3.87 us (4%)
    pallas_call x1, Pallas kernels, project(): pl.pallas_call(functools.partial(project_kernel, seq_count, chan_count),...  41.4 us
    pallas_call x1, Pallas kernels, project_out(): pl.pallas_call(functools.partial(output_kernel, seq_count, chan_count), o...  32.8 us
    pallas_call x1, Pallas kernels, mix(): pl.pallas_call(functools.partial(mix_kernel, gsize), grid=(chans // LANES...  8.57 us
    unnamed x9, local copies, waits for them, and re-layouts  1.85 us

profile of v4, /device:TPU:13, one launch (start us, length us, event | category | flops | bytes accessed | tf_op | source)
XLA Modules:
  0.0 87.7 jit_solution(4398842660692080580)
XLA Ops:
  0.0 0.0 copy-start.3
  0.0 0.0 copy-start.2
  0.1 0.8 pad_dynamic-slice_fusion
  0.9 0.1 slice.16
  1.0 0.1 slice.14
  1.0 0.1 fusion.10
  1.1 0.1 pad_maximum_fusion
  1.2 0.8 rev.3
  2.0 0.1 pad_convert_fusion.pattern
  2.1 0.5 fusion.4.fold
  2.7 0.1 copy.12.seg_col
  2.8 0.1 copy.11.near
  3.0 0.0 copy-start.1
  3.0 1.0 %copy-done.1 = bf16[256,1024]{1,0:T(8,128)(2,1)S(1)} copy-done((bf16[256,1024]{1,0:T(8,128)(2,1)S(1)}, bf16[256,1024]{1,0:T(8,128)(2,1)}, u32[]{:S(2)}) %copy-start.1) | copy-done | bytes 524312
  4.0 0.0 copy-start
  4.0 41.4 %shard_map.73 = (bf16[256,1024]{1,0:T(8,128)(2,1)S(1)}, bf16[256,1024]{1,0:T(8,128)(2,1)S(1)}, bf16[256,1024]{1,0:T(8,128)(2,1)S(1)}, bf16[16,1024]{1,0:T(8,128)...) custom-call(bf16[256,1024]{1,0:T(8,128)(2,1)S(1)} %copy-done.1, bf16[3,4096,1024]{2,1,0:T(8,128)(2,1)} %bitcast.5, ...), custom_call_target="tpu_custom_call" | custom-call | tf_op jit(solution)/shard_map/pallas_call | solution.py:290
  45.5 0.0 copy-done.3
  45.5 0.0 copy-done.2
  45.5 8.6 %shard_map.74.folded = bf16[256,1024]{1,0:T(8,128)(2,1)S(1)} custom-call(bf16[256,1024]{1,0:T(8,128)(2,1)S(1)} %get-tuple-element.11.q, bf16[256,1024]{1,0:T(8,128)(2,1)S(1)} %get-tuple-element.12.k, bf16[256,1024]{1,0:T(8,128)(2,1)S(1)} %get-tuple-element.13.v, bf16[16,1024]{1,0:T(8,128)(2,1)S(1)} %get-tuple-element.14.hq, ...), custom_call_target="tpu_custom_call" | custom-call | tf_op jit(solution)/shard_map/pallas_call | solution.py:91
  54.1 0.0 copy-done
  54.1 32.8 %shard_map.75 = bf16[256,1024]{1,0:T(8,128)(2,1)S(1)} custom-call(bf16[256,1024]{1,0:T(8,128)(2,1)S(1)} %shard_map.74.folded, bf16[1024,4096]{1,0:T(8,128)(2,1)S(1)} %copy-done), custom_call_target="tpu_custom_call" | custom-call | tf_op jit(solution)/shard_map/pallas_call | solution.py:393
  86.9 0.8 copy.14
  (15 shorter events, 0.1 us)
Async XLA Ops:
  0.0 45.5 %copy-start.3 = (f32[1024]{0:T(1024)S(1)}, f32[1024]{0:T(1024)}, u32[]{:S(2)}) copy-start(f32[1024]{0:T(1024)} %param.11) | copy-start | bytes 12292
  0.0 45.5 %copy-start.2 = (f32[3,3,1024]{2,1,0:T(4,128)S(1)}, f32[3,3,1024]{2,1,0:T(4,128)}, u32[]{:S(2)}) copy-start(f32[3,3,1024]{2,1,0:T(4,128)} %short.1) | copy-start | bytes 110596
  3.0 1.0 %copy-start.1 = (bf16[256,1024]{1,0:T(8,128)(2,1)S(1)}, bf16[256,1024]{1,0:T(8,128)(2,1)}, u32[]{:S(2)}) copy-start(bf16[256,1024]{1,0:T(8,128)(2,1)} %tokens.1) | copy-start | bytes 1572868
  4.0 50.0 %copy-start = (bf16[1024,4096]{1,0:T(8,128)(2,1)S(1)}, bf16[1024,4096]{1,0:T(8,128)(2,1)}, u32[]{:S(2)}) copy-start(bf16[1024,4096]{1,0:T(8,128)(2,1)} %w.1) | copy-start | bytes 25165828

commit v5 on v4

--- a/solution.py
+++ b/solution.py
@@ -177,7 +177,7 @@
     rows, width = tokens.shape
     half_rows = rows // 2
     f32 = jnp.float32
-    tile = min(256, wbuf.shape[2])
+    tile = min(512, wbuf.shape[2])
     tiles = wbuf.shape[2] // tile
 
     uses = [chip * 2 + core, chip * 2 + 1 - core]
@@ -320,7 +320,7 @@
     rows_to, across, sibling = partners(seq, chip, core, seq_count, chips)
     f32 = jnp.float32
     width = out.shape[1]
-    tile = min(256, width)
+    tile = min(512, width)
     load = pltpu.make_async_copy(w, wbuf, w_sem)
     load.start()
     greet(rows_to + across + [sibling])

time: 88.2 us -> 85.1 us (0.965)
  Pallas kernels: 82.8 us -> 79.7 us
    pallas_call x1, Pallas kernels: 41.4 us -> 38.9 us  [project(): pl.pallas_call(functools.partial(project_kernel, seq_count, chan_count),...]
where the time goes in v5:
time: 85.1 us; the launch traced here: 84.5 us
  Pallas kernels  79.7 us (94%)
  local copies, waits for them, and re-layouts  3.87 us (5%)
    pallas_call x1, Pallas kernels, project(): pl.pallas_call(functools.partial(project_kernel, seq_count, chan_count),...  38.9 us
    pallas_call x1, Pallas kernels, project_out(): pl.pallas_call(functools.partial(output_kernel, seq_count, chan_count), o...  32.1 us
    pallas_call x1, Pallas kernels, mix(): pl.pallas_call(functools.partial(mix_kernel, gsize), grid=(chans // LANES...  8.57 us
    unnamed x9, local copies, waits for them, and re-layouts  1.85 us

profile of v5, /device:TPU:13, one launch (start us, length us, event | category | flops | bytes accessed | tf_op | source)
XLA Modules:
  0.0 84.5 jit_solution(12718054467321666011)
XLA Ops:
  0.0 0.0 copy-start.3
  0.0 0.0 copy-start.2
  0.1 0.8 pad_dynamic-slice_fusion
  0.9 0.1 slice.16
  1.0 0.1 slice.14
  1.0 0.1 fusion.10
  1.1 0.1 pad_maximum_fusion
  1.2 0.8 rev.3
  2.0 0.1 pad_convert_fusion.pattern
  2.1 0.5 fusion.4.fold
  2.7 0.1 copy.12.seg_col
  2.8 0.1 copy.11.near
  3.0 0.0 copy-start.1
  3.0 1.0 %copy-done.1 = bf16[256,1024]{1,0:T(8,128)(2,1)S(1)} copy-done((bf16[256,1024]{1,0:T(8,128)(2,1)S(1)}, bf16[256,1024]{1,0:T(8,128)(2,1)}, u32[]{:S(2)}) %copy-start.1) | copy-done | bytes 524312
  4.0 0.0 copy-start
  4.0 38.9 %shard_map.73 = (bf16[256,1024]{1,0:T(8,128)(2,1)S(1)}, bf16[256,1024]{1,0:T(8,128)(2,1)S(1)}, bf16[256,1024]{1,0:T(8,128)(2,1)S(1)}, bf16[16,1024]{1,0:T(8,128)...) custom-call(bf16[256,1024]{1,0:T(8,128)(2,1)S(1)} %copy-done.1, bf16[3,4096,1024]{2,1,0:T(8,128)(2,1)} %bitcast.5, ...), custom_call_target="tpu_custom_call" | custom-call | tf_op jit(solution)/shard_map/pallas_call | solution.py:290
  43.0 0.0 copy-done.3
  43.0 0.0 copy-done.2
  43.0 8.6 %shard_map.74.folded = bf16[256,1024]{1,0:T(8,128)(2,1)S(1)} custom-call(bf16[256,1024]{1,0:T(8,128)(2,1)S(1)} %get-tuple-element.11.q, bf16[256,1024]{1,0:T(8,128)(2,1)S(1)} %get-tuple-element.12.k, bf16[256,1024]{1,0:T(8,128)(2,1)S(1)} %get-tuple-element.13.v, bf16[16,1024]{1,0:T(8,128)(2,1)S(1)} %get-tuple-element.14.hq, ...), custom_call_target="tpu_custom_call" | custom-call | tf_op jit(solution)/shard_map/pallas_call | solution.py:91
  51.6 0.0 copy-done
  51.6 32.1 %shard_map.75 = bf16[256,1024]{1,0:T(8,128)(2,1)S(1)} custom-call(bf16[256,1024]{1,0:T(8,128)(2,1)S(1)} %shard_map.74.folded, bf16[1024,4096]{1,0:T(8,128)(2,1)S(1)} %copy-done), custom_call_target="tpu_custom_call" | custom-call | tf_op jit(solution)/shard_map/pallas_call | solution.py:393
  83.7 0.8 copy.14
  (15 shorter events, 0.1 us)
Async XLA Ops:
  0.0 43.0 %copy-start.3 = (f32[1024]{0:T(1024)S(1)}, f32[1024]{0:T(1024)}, u32[]{:S(2)}) copy-start(f32[1024]{0:T(1024)} %param.11) | copy-start | bytes 12292
  0.0 43.0 %copy-start.2 = (f32[3,3,1024]{2,1,0:T(4,128)S(1)}, f32[3,3,1024]{2,1,0:T(4,128)}, u32[]{:S(2)}) copy-start(f32[3,3,1024]{2,1,0:T(4,128)} %short.1) | copy-start | bytes 110596
  3.0 1.0 %copy-start.1 = (bf16[256,1024]{1,0:T(8,128)(2,1)S(1)}, bf16[256,1024]{1,0:T(8,128)(2,1)}, u32[]{:S(2)}) copy-start(bf16[256,1024]{1,0:T(8,128)(2,1)} %tokens.1) | copy-start | bytes 1572868
  4.0 47.6 %copy-start = (bf16[1024,4096]{1,0:T(8,128)(2,1)S(1)}, bf16[1024,4096]{1,0:T(8,128)(2,1)}, u32[]{:S(2)}) copy-start(bf16[1024,4096]{1,0:T(8,128)(2,1)} %w.1) | copy-start | bytes 25165828
